TPU v7x, 512 devices: a whole 4x8x8 slice. The times are simulated.
512 devices in a mesh: list: 16 (over z, core), sub: 8 (over y), slab: 4 (over x).
Axes of the slice: x: 4, y: 8, z: 8, core: 2. Of those that a mesh axis runs over, the one named last changes fastest.
Arguments:
- vectors: float32 [1024, 65536], P(None, ('list', 'sub', 'slab')), may hold values from -10 to 10
- centroids: bfloat16 [1024, 262144], P('sub', ('list', 'slab')), may hold values from -3 to 3
- codebook: float32 [32, 256, 32], P('sub'), may hold values from -10 to 10
- list_ids: int32 [65536], P(('list', 'sub', 'slab')), may hold values from 0 to 262143, as said below
Outputs:
- fresh_codebook: float32 [32, 256, 32], P('sub')
Inputs may be any that keep to these rules, and one draw needn't show every extreme that they name: `list_ids`: among the columns of one device, at most 4 name lists of one owner (list id // 4096); in every draw one owner receives exactly 4 from every device.
All inputs are finite; a program needn't handle non-finite values.
Results may differ from a plain program's by a relative error of at most 0.0003.
Values sent between devices are 32-bit elements; how exact they have to be, the bound alone decides.
A program may use at most 64 MiB of HBM per device.

v0:
```python
import math
import jax
import jax.numpy as jnp
from jax import lax
from jax.sharding import PartitionSpec as P

SOFTMAX_HEAT = 8.0
PRIOR_MASS = 1.0


def owner_rank(owner_of, owners):
    row_count = owner_of.shape[0]
    matches = (owner_of[:, None] == jnp.arange(owners)[None, :]).astype(jnp.float32)
    block = math.gcd(row_count, 128)
    blocks = matches.reshape(row_count // block, block, owners)
    strict_lower = (jnp.arange(block)[:, None] > jnp.arange(block)[None, :]).astype(jnp.float32)
    inside = jnp.einsum("ij,bjo->bio", strict_lower, blocks)
    totals = jnp.sum(blocks, axis=1)
    before = jnp.cumsum(totals, axis=0) - totals
    ranking = (inside + before[:, None, :]).reshape(row_count, owners)
    return jnp.sum(ranking * matches, axis=1).astype(jnp.int32)


def soft_sums(residual, weight, codebook):
    groups, num_codes, width = codebook.shape
    total_columns = residual.shape[1]
    block = math.gcd(total_columns, 1024)
    codeword_norm = jnp.sum(codebook * codebook, axis=-1)

    def block_step(loop_index, running):
        counts, weighted = running
        offset = (loop_index * block).astype(jnp.int32)
        column_piece = lax.dynamic_slice_in_dim(residual, offset, block, 1).reshape(
            groups, width, block
        )
        present = lax.dynamic_slice_in_dim(weight, offset, block, 0)
        inner_products = jnp.einsum(
            "skd,sdn->skn", codebook, column_piece, precision=lax.Precision.HIGHEST
        )
        assignment_scores = (2.0 * inner_products - codeword_norm[:, :, None]) / SOFTMAX_HEAT
        assignment_scores = assignment_scores - jnp.max(assignment_scores, axis=1, keepdims=True)
        exponent = jnp.exp(assignment_scores)
        assign = exponent / jnp.sum(exponent, axis=1, keepdims=True) * present[None, None, :]
        counts = counts + jnp.sum(assign, axis=2)
        weighted = weighted + jnp.einsum(
            "skn,sdn->skd", assign, column_piece, precision=lax.Precision.HIGHEST
        )
        return (counts, weighted)

    start_state = (
        jnp.zeros((groups, num_codes), jnp.float32),
        jnp.zeros((groups, num_codes, width), jnp.float32),
    )
    return lax.fori_loop(0, total_columns // block, block_step, start_state)


def refresh(counts, weighted, previous):
    return (weighted + PRIOR_MASS * previous) / (counts[:, :, None] + PRIOR_MASS)


def per_device(vectors, centroids, codebook, list_ids):
    list_count = lax.axis_size("list")
    slab_count = lax.axis_size("slab")
    sub_count = lax.axis_size("sub")
    owners = list_count * slab_count
    lists_here = centroids.shape[1]
    row_count = vectors.shape[1]
    capacity = 2 * row_count // owners
    owner_of = list_ids // lists_here
    within = (list_ids % lists_here).astype(jnp.float32)
    slot = owner_of * capacity + owner_rank(owner_of, owners)
    packed = jnp.zeros((vectors.shape[0], owners * capacity), jnp.float32).at[:, slot].set(vectors)
    labels = jnp.full((owners * capacity,), -1.0, jnp.float32).at[slot].set(within)
    labels = jnp.broadcast_to(labels[None, :], (sub_count, owners * capacity))
    arrived, arrived_labels = (
        lax.all_to_all(packed, ("list", "slab"), split_axis=1, concat_axis=1, tiled=True),
        lax.all_to_all(labels, ("list", "slab"), split_axis=1, concat_axis=1, tiled=True),
    )
    columns, column_labels = (
        lax.all_to_all(arrived, "sub", split_axis=0, concat_axis=1, tiled=True),
        lax.all_to_all(arrived_labels, "sub", split_axis=0, concat_axis=1, tiled=True),
    )
    final_labels = column_labels[0]
    present = final_labels >= 0.0
    weight = present.astype(jnp.float32)
    list_index = jnp.where(present, final_labels, 0.0).astype(jnp.int32)
    nearest = jnp.take(centroids, list_index, axis=1).astype(jnp.float32)
    residual = (columns - nearest) * weight[None, :]
    counts, weighted = soft_sums(residual, weight, codebook)
    counts, weighted = lax.psum((counts, weighted), ("list", "slab"))
    return refresh(counts, weighted, codebook)


def solution(mesh):
    return jax.shard_map(
        per_device,
        mesh=mesh,
        in_specs=(
            P(None, ("list", "sub", "slab")),
            P("sub", ("list", "slab")),
            P("sub", None, None),
            P(("list", "sub", "slab")),
        ),
        out_specs=P("sub", None, None),
        check_vma=False,
    )
```

profile of v0, /device:TPU:1, one launch (start us, length us, event | category | flops | bytes accessed | tf_op | source)
XLA Modules:
  0.0 453.4 jit_solution(12421118974912579844)
XLA Ops:
  6.5 0.7 fusion.23
  7.2 0.1 convert_reduce_fusion
  7.3 0.2 fusion.16
  7.5 1.0 scatter_custom_fusion.1
  8.5 0.1 broadcast_in_dim.60
  8.6 0.8 broadcast_in_dim.61
  9.4 14.8 %all-to-all-start.2 = ((f32[8,64,4]{0,2,1:T(4,128)}), f32[8,64,4]{0,2,1:T(4,128)S(1)}, u32[]{:S(2)}, u32[]{:S(2)}) async-start(f32[8,64,4]{0,2,1:T(4,128)} %broadcast_in_dim.61), calls=%async_computation.2 | async-start | bytes 262144 | tf_op jit(solution)/shard_map/all_to_all | solution.py:77
  24.2 1.2 copy.24
  25.5 1.3 scatter_custom_fusion
  26.8 1.3 all_to_all.34
  28.1 0.0 copy-start.2
  28.1 6.1 %all-to-all-done.2 = f32[8,64,4]{0,2,1:T(4,128)S(1)} async-done(((f32[8,64,4]{0,2,1:T(4,128)}), f32[8,64,4]{0,2,1:T(4,128)S(1)}, u32[]{:S(2)}, u32[]{:S(2)}) %all-to-all-start.2) | async-done | bytes 8224 | tf_op jit(solution)/shard_map/all_to_all | solution.py:77
  34.2 6.0 %all-to-all-start = ((f32[1024,64,4]{0,2,1:T(4,128)}), f32[1024,64,4]{0,2,1:T(4,128)S(1)}, u32[]{:S(2)}, u32[]{:S(2)}) async-start(f32[1024,64,4]{0,2,1:T(4,128)} %all_to_all.34), calls=%async_computation | async-start | bytes 2097152 | tf_op jit(solution)/shard_map/all_to_all | solution.py:76
  40.2 0.7 copy.26
  40.8 27.1 %all-to-all-done = f32[1024,64,4]{0,2,1:T(4,128)S(1)} async-done(((f32[1024,64,4]{0,2,1:T(4,128)}), f32[1024,64,4]{0,2,1:T(4,128)S(1)}, u32[]{:S(2)}, u32[]{:S(2)}) %all-to-all-start) | async-done | bytes 1048608 | tf_op jit(solution)/shard_map/all_to_all | solution.py:76
  68.0 6.8 %all-to-all-start.3 = ((f32[8,1,256]{2,1,0:T(1,128)}), f32[8,1,256]{2,1,0:T(1,128)S(1)}, u32[]{:S(2)}, u32[]{:S(2)}) async-start(f32[8,1,256]{2,1,0:T(1,128)} %copy.26), calls=%async_computation.3 | async-start | bytes 16384 | tf_op jit(solution)/shard_map/all_to_all | solution.py:81
  74.8 0.0 copy-start.1
  74.8 0.4 all_to_all.36
  75.2 1.2 copy.25
  76.4 5.0 %all-to-all-done.3 = f32[8,1,256]{2,1,0:T(1,128)S(1)} async-done(((f32[8,1,256]{2,1,0:T(1,128)}), f32[8,1,256]{2,1,0:T(1,128)S(1)}, u32[]{:S(2)}, u32[]{:S(2)}) %all-to-all-start.3) | async-done | bytes 8224 | tf_op jit(solution)/shard_map/all_to_all | solution.py:81
  81.4 3.6 all-to-all-start.1
  84.9 0.2 all-reduce.2.cloned.1.call-start
  85.2 0.0 copy-done.2
  85.2 0.7 copy.27
  85.8 0.0 copy-done.1
  85.9 6.2 %gather_fusion = bf16[2048,128]{1,0:T(8,128)(2,1)S(1)} fusion(bf16[128,4096]{0,1:T(8,128)(2,1)S(1)} %copy.27, s32[2048]{0:T(1024)S(1)} %broadcast_clamp_fusion), kind=kCustom, calls=%fused_computation | custom fusion | bytes 1056768 | tf_op jit(solution)/shard_map/jit(_take)/gather | solution.py:87
  92.1 19.6 %all-to-all-done.1 = f32[8,128,256]{1,2,0:T(8,128)S(1)} async-done(((f32[8,128,256]{1,2,0:T(8,128)}), f32[8,128,256]{1,2,0:T(8,128)S(1)}, u32[]{:S(2)}, u32[]{:S(2)}) %all-to-all-start.1) | async-done | bytes 1048608 | tf_op jit(solution)/shard_map/all_to_all | solution.py:80
  111.7 0.8 fusion.17
  112.5 27.6 %while.16 = (s32[]{:T(128)}, f32[4,256]{1,0:T(4,128)S(1)}, f32[4,256,32]{1,2,0:T(8,128)S(1)}, f32[128,2048]{0,1:T(8,128)S(1)}, f32[4,256,32]{1,2,0:T(8,128)S(1)}...) while((s32[]{:T(128)}, f32[4,256]{1,0:T(4,128)S(1)}, ...), condition=%wide.region_9.10_spmd.clone, body=%wide.region_5.9_spmd.clone.sunk | while | flops 819004672 | bytes 41373896 | solution.py:54
  112.6 0.2 copy.31
  112.8 3.5 fusion.41
  116.2 3.0 fusion.42
  119.2 0.0 copy-start
  119.2 6.5 %fusion.44 = f32[4,256,32]{1,2,0:T(8,128)S(1)} fusion(f32[4,32,1024]{2,1,0:T(8,128)S(1)} %bitcast.61, f32[4,256,1024]{2,1,0:T(8,128)} %get-tuple-element.256, f32[1024]{0:T(1024)S(1)} %dynamic_slice.20, f32[4,1024]{1,0:T(4,128)S(1)} %get-tuple-element.257, f32[4,256,32]{1,2,0:T(8,128)S(1)} %get-tuple-element.271, pred[]{:T(512)S(6)} %compare.6), kind=kOutput, calls=%fused_computation.15.clone.1 | convolution fusion | flops 404815872 | bytes 5001217 | tf_op jit(solution)/shard_map/while/body/eval_jaxpr/skn,sdn->skd/dot_general | solution.py:45
  125.8 0.0 copy-done
  125.8 0.5 fusion.43
  126.4 0.2 copy.31
  126.6 3.5 fusion.41
  130.0 3.0 fusion.42
  133.0 0.0 copy-start
  133.0 6.5 %fusion.44 = f32[4,256,32]{1,2,0:T(8,128)S(1)} fusion(f32[4,32,1024]{2,1,0:T(8,128)S(1)} %bitcast.61, f32[4,256,1024]{2,1,0:T(8,128)} %get-tuple-element.256, f32[1024]{0:T(1024)S(1)} %dynamic_slice.20, f32[4,1024]{1,0:T(4,128)S(1)} %get-tuple-element.257, f32[4,256,32]{1,2,0:T(8,128)S(1)} %get-tuple-element.271, pred[]{:T(512)S(6)} %compare.6), kind=kOutput, calls=%fused_computation.15.clone.1 | convolution fusion | flops 404815872 | bytes 5001217 | tf_op jit(solution)/shard_map/while/body/eval_jaxpr/skn,sdn->skd/dot_general | solution.py:45
  139.6 0.0 copy-done
  139.6 0.5 fusion.43
  140.1 0.0 copy-start.3
  140.1 123.2 %psum.15 = f32[4,256]{1,0:T(4,128)S(1)} all-reduce(f32[4,256]{1,0:T(4,128)S(1)} %get-tuple-element.131), channel_id=1, replica_groups=mesh['list'=16,'sub'=8,'slab'=4] {'list','slab'}, use_global_device_ids=true, to_apply=%region_11.12 | all-reduce | flops 1024 | bytes 8192 | tf_op jit(solution)/shard_map/psum | solution.py:90
  263.3 0.0 copy-done.3
  263.3 0.0 all-reduce.2.cloned.1.call-update
  263.4 181.7 %all-reduce.2.cloned.1.call-done = f32[4,256,32]{1,2,0:T(8,128)} async-done(((f32[4,256,32]{1,2,0:T(8,128)}), f32[4,256,32]{1,2,0:T(8,128)}) %all-reduce.2.cloned.1.call-update) | async-done | bytes 131088 | tf_op jit(solution)/shard_map/psum | solution.py:90
  445.0 1.6 add_divide_fusion
  (15 shorter events, 0.2 us)
Async XLA Ops:
  9.4 24.8 %all-to-all-start.2 = ((f32[8,64,4]{0,2,1:T(4,128)}), f32[8,64,4]{0,2,1:T(4,128)S(1)}, u32[]{:S(2)}, u32[]{:S(2)}) async-start(f32[8,64,4]{0,2,1:T(4,128)} %broadcast_in_dim.61), calls=%async_computation.2 | async-start | bytes 262144 | tf_op jit(solution)/shard_map/all_to_all | solution.py:77
  28.1 57.1 %copy-start.2 = (bf16[128,4096]{1,0:T(8,128)(2,1)S(1)}, bf16[128,4096]{1,0:T(8,128)(2,1)}, u32[]{:S(2)}) copy-start(bf16[128,4096]{1,0:T(8,128)(2,1)} %param.7) | copy-start | bytes 3145732
  34.2 33.8 %all-to-all-start = ((f32[1024,64,4]{0,2,1:T(4,128)}), f32[1024,64,4]{0,2,1:T(4,128)S(1)}, u32[]{:S(2)}, u32[]{:S(2)}) async-start(f32[1024,64,4]{0,2,1:T(4,128)} %all_to_all.34), calls=%async_computation | async-start | bytes 2097152 | tf_op jit(solution)/shard_map/all_to_all | solution.py:76
  68.0 13.4 %all-to-all-start.3 = ((f32[8,1,256]{2,1,0:T(1,128)}), f32[8,1,256]{2,1,0:T(1,128)S(1)}, u32[]{:S(2)}, u32[]{:S(2)}) async-start(f32[8,1,256]{2,1,0:T(1,128)} %copy.26), calls=%async_computation.3 | async-start | bytes 16384 | tf_op jit(solution)/shard_map/all_to_all | solution.py:81
  74.8 11.1 %copy-start.1 = (f32[4,256,32]{1,2,0:T(8,128)S(1)}, f32[4,256,32]{1,2,0:T(8,128)}, u32[]{:S(2)}) copy-start(f32[4,256,32]{1,2,0:T(8,128)} %param.8) | copy-start | bytes 393220
  81.4 30.4 %all-to-all-start.1 = ((f32[8,128,256]{1,2,0:T(8,128)}), f32[8,128,256]{1,2,0:T(8,128)S(1)}, u32[]{:S(2)}, u32[]{:S(2)}) async-start(f32[8,128,256]{1,2,0:T(8,128)} %copy.25), calls=%async_computation.1 | async-start | bytes 2097152 | tf_op jit(solution)/shard_map/all_to_all | solution.py:80
  84.9 360.1 %all-reduce.2.cloned.1.call-start = ((), (), s32[]{:S(2)}) async-start(), calls=%async_computation.4 | async-start | bytes 262144 | tf_op jit(solution)/shard_map/psum | solution.py:90
  119.2 6.5 %copy-start = (f32[4,256,1024]{2,1,0:T(8,128)S(1)}, f32[4,256,1024]{2,1,0:T(8,128)}, u32[]{:S(2)}) copy-start(f32[4,256,1024]{2,1,0:T(8,128)} %get-tuple-element.256) | copy-start | bytes 12582916 | tf_op jit(solution)/shard_map/while
  133.0 6.5 %copy-start = (f32[4,256,1024]{2,1,0:T(8,128)S(1)}, f32[4,256,1024]{2,1,0:T(8,128)}, u32[]{:S(2)}) copy-start(f32[4,256,1024]{2,1,0:T(8,128)} %get-tuple-element.256) | copy-start | bytes 12582916 | tf_op jit(solution)/shard_map/while
  140.1 123.2 %copy-start.3 = (f32[4,256,32]{1,2,0:T(8,128)}, f32[4,256,32]{1,2,0:T(8,128)S(1)}, u32[]{:S(2)}) copy-start(f32[4,256,32]{1,2,0:T(8,128)S(1)} %get-tuple-element.130) | copy-start | bytes 393220
Sparse Core Ops, SparseCore 0:
  263.5 181.4 all-reduce.1
where the time goes:
time: 454 us; the launch traced here: 453 us
  waiting for transfers between devices  239 us (53%)
  blocking collectives  123 us (27%)
  starting transfers between devices  31.4 us (7%)
  matrix products  20.1 us (4%)
  local copies, waits for them, and re-layouts  15.3 us (3%)
  between operations  13.6 us (3%)
  other arithmetic  10.2 us (2%)
    psum x1, waiting for transfers between devices, per_device(): counts, weighted = lax.psum((counts, weighted), ('list', 'slab'))  182 us
    psum x1, blocking collectives, per_device(): counts, weighted = lax.psum((counts, weighted), ('list', 'slab'))  123 us
    all_to_all x1, waiting for transfers between devices, per_device(): lax.all_to_all(packed, ('list', 'slab'), split_axis=1, concat_axis=1, til...  27.1 us
    all_to_all x1, waiting for transfers between devices, per_device(): lax.all_to_all(arrived, 'sub', split_axis=0, concat_axis=1, tiled=True)  19.6 us
    all_to_all x1, starting transfers between devices, per_device(): lax.all_to_all(labels, ('list', 'slab'), split_axis=1, concat_axis=1, til...  14.8 us
    dot_general x2, matrix products, block_step(): jnp.einsum('skn,sdn->skd', assign, column_piece, precision=lax.Precision....  13 us
  transfers between devices with their start and end apart: 5, of which 5 were waited for; matrix products, arithmetic and copies ran while one was open for 2% of the time, Pallas kernels for 0%

commit v1 on v0

--- a/solution.py
+++ b/solution.py
@@ -87,7 +87,7 @@
     nearest = jnp.take(centroids, list_index, axis=1).astype(jnp.float32)
     residual = (columns - nearest) * weight[None, :]
     counts, weighted = soft_sums(residual, weight, codebook)
-    counts, weighted = lax.psum((counts, weighted), ("list", "slab"))
+    counts, weighted = lax.psum(lax.psum((counts, weighted), "slab"), "list")
     return refresh(counts, weighted, codebook)
 
 

time: 454 us -> 313 us (0.69)
  blocking collectives: 123 us -> 36.5 us
  waiting for transfers between devices: 239 us -> 185 us
    psum x1 -> x2, blocking collectives: 123 us -> 36.5 us  [per_device(): counts, weighted = lax.psum(lax.psum((counts, weighted), 'slab'), 'list')]
    psum x1 -> x2, waiting for transfers between devices: 182 us -> 127 us  [per_device(): counts, weighted = lax.psum(lax.psum((counts, weighted), 'slab'), 'list')]
  transfers between devices with their start and end apart: 5 -> 6, of which waited for: 5 -> 6; matrix products, arithmetic and copies ran while one was open for 2% -> 4% of each run, Pallas kernels for 0% -> 0%
where the time goes in v1:
time: 313 us; the launch traced here: 312 us
  waiting for transfers between devices  185 us (59%)
  blocking collectives  36.5 us (12%)
  starting transfers between devices  31.5 us (10%)
  matrix products  20.1 us (6%)
  local copies, waits for them, and re-layouts  15.9 us (5%)
  between operations  13.6 us (4%)
  other arithmetic  10.2 us (3%)
    psum x2, waiting for transfers between devices, per_device(): counts, weighted = lax.psum(lax.psum((counts, weighted), 'slab'), 'list')  127 us
    psum x2, blocking collectives, per_device(): counts, weighted = lax.psum(lax.psum((counts, weighted), 'slab'), 'list')  36.5 us
    all_to_all x1, waiting for transfers between devices, per_device(): lax.all_to_all(packed, ('list', 'slab'), split_axis=1, concat_axis=1, til...  27.1 us
    all_to_all x1, waiting for transfers between devices, per_device(): lax.all_to_all(arrived, 'sub', split_axis=0, concat_axis=1, tiled=True)  19.6 us
    all_to_all x1, starting transfers between devices, per_device(): lax.all_to_all(labels, ('list', 'slab'), split_axis=1, concat_axis=1, til...  14.8 us
    dot_general x2, matrix products, block_step(): jnp.einsum('skn,sdn->skd', assign, column_piece, precision=lax.Precision....  13 us
    dot_general x2, matrix products, block_step(): jnp.einsum('skd,sdn->skn', codebook, column_piece, precision=lax.Precisio...  6.92 us
    all_to_all x1, starting transfers between devices, per_device(): lax.all_to_all(arrived_labels, 'sub', split_axis=0, concat_axis=1, tiled=...  6.82 us
  transfers between devices with their start and end apart: 6, of which 6 were waited for; matrix products, arithmetic and copies ran while one was open for 4% of the time, Pallas kernels for 0%

profile of v1, /device:TPU:1, one launch (start us, length us, event | category | flops | bytes accessed | tf_op | source)
XLA Modules:
  0.0 312.5 jit_solution(11920723356979781612)
XLA Ops:
  6.5 0.7 fusion.23
  7.2 0.1 convert_reduce_fusion
  7.3 0.2 fusion.16
  7.5 1.0 scatter_custom_fusion.1
  8.5 0.1 broadcast_in_dim.60
  8.6 0.8 broadcast_in_dim.61
  9.4 14.8 %all-to-all-start.2 = ((f32[8,64,4]{0,2,1:T(4,128)}), f32[8,64,4]{0,2,1:T(4,128)S(1)}, u32[]{:S(2)}, u32[]{:S(2)}) async-start(f32[8,64,4]{0,2,1:T(4,128)} %broadcast_in_dim.61), calls=%async_computation.2 | async-start | bytes 262144 | tf_op jit(solution)/shard_map/all_to_all | solution.py:77
  24.2 1.2 copy.24
  25.5 1.3 scatter_custom_fusion
  26.8 1.3 all_to_all.34
  28.1 0.0 copy-start.2
  28.1 6.1 %all-to-all-done.2 = f32[8,64,4]{0,2,1:T(4,128)S(1)} async-done(((f32[8,64,4]{0,2,1:T(4,128)}), f32[8,64,4]{0,2,1:T(4,128)S(1)}, u32[]{:S(2)}, u32[]{:S(2)}) %all-to-all-start.2) | async-done | bytes 8224 | tf_op jit(solution)/shard_map/all_to_all | solution.py:77
  34.2 6.0 %all-to-all-start = ((f32[1024,64,4]{0,2,1:T(4,128)}), f32[1024,64,4]{0,2,1:T(4,128)S(1)}, u32[]{:S(2)}, u32[]{:S(2)}) async-start(f32[1024,64,4]{0,2,1:T(4,128)} %all_to_all.34), calls=%async_computation | async-start | bytes 2097152 | tf_op jit(solution)/shard_map/all_to_all | solution.py:76
  40.2 0.7 copy.26
  40.8 27.1 %all-to-all-done = f32[1024,64,4]{0,2,1:T(4,128)S(1)} async-done(((f32[1024,64,4]{0,2,1:T(4,128)}), f32[1024,64,4]{0,2,1:T(4,128)S(1)}, u32[]{:S(2)}, u32[]{:S(2)}) %all-to-all-start) | async-done | bytes 1048608 | tf_op jit(solution)/shard_map/all_to_all | solution.py:76
  68.0 6.8 %all-to-all-start.3 = ((f32[8,1,256]{2,1,0:T(1,128)}), f32[8,1,256]{2,1,0:T(1,128)S(1)}, u32[]{:S(2)}, u32[]{:S(2)}) async-start(f32[8,1,256]{2,1,0:T(1,128)} %copy.26), calls=%async_computation.3 | async-start | bytes 16384 | tf_op jit(solution)/shard_map/all_to_all | solution.py:81
  74.8 0.0 copy-start.1
  74.8 0.4 all_to_all.36
  75.2 1.2 copy.25
  76.4 5.0 %all-to-all-done.3 = f32[8,1,256]{2,1,0:T(1,128)S(1)} async-done(((f32[8,1,256]{2,1,0:T(1,128)}), f32[8,1,256]{2,1,0:T(1,128)S(1)}, u32[]{:S(2)}, u32[]{:S(2)}) %all-to-all-start.3) | async-done | bytes 8224 | tf_op jit(solution)/shard_map/all_to_all | solution.py:81
  81.4 3.6 %all-to-all-start.1 = ((f32[8,128,256]{1,2,0:T(8,128)}), f32[8,128,256]{1,2,0:T(8,128)S(1)}, u32[]{:S(2)}, u32[]{:S(2)}) async-start(f32[8,128,256]{1,2,0:T(8,128)} %copy.25), calls=%async_computation.1 | async-start | bytes 2097152 | tf_op jit(solution)/shard_map/all_to_all | solution.py:80
  84.9 0.2 all-reduce.3.cloned.1.call-start
  85.2 0.0 copy-done.2
  85.2 0.7 copy.27
  85.8 0.0 copy-done.1
  85.9 6.2 %gather_fusion = bf16[2048,128]{1,0:T(8,128)(2,1)S(1)} fusion(bf16[128,4096]{0,1:T(8,128)(2,1)S(1)} %copy.27, s32[2048]{0:T(1024)S(1)} %broadcast_clamp_fusion), kind=kCustom, calls=%fused_computation | custom fusion | bytes 1056768 | tf_op jit(solution)/shard_map/jit(_take)/gather | solution.py:87
  92.1 19.6 %all-to-all-done.1 = f32[8,128,256]{1,2,0:T(8,128)S(1)} async-done(((f32[8,128,256]{1,2,0:T(8,128)}), f32[8,128,256]{1,2,0:T(8,128)S(1)}, u32[]{:S(2)}, u32[]{:S(2)}) %all-to-all-start.1) | async-done | bytes 1048608 | tf_op jit(solution)/shard_map/all_to_all | solution.py:80
  111.7 0.8 fusion.17
  112.5 27.6 %while.16 = (s32[]{:T(128)}, f32[4,256]{1,0:T(4,128)S(1)}, f32[4,256,32]{1,2,0:T(8,128)S(1)}, f32[128,2048]{0,1:T(8,128)S(1)}, f32[4,256,32]{1,2,0:T(8,128)S(1)}...) while((s32[]{:T(128)}, f32[4,256]{1,0:T(4,128)S(1)}, ...), condition=%wide.region_9.10_spmd.clone, body=%wide.region_5.9_spmd.clone.sunk | while | flops 819004672 | bytes 41373896 | solution.py:54
  112.6 0.2 copy.31
  112.8 3.5 %fusion.41 = f32[4,1024,256]{1,2,0:T(8,128)S(1)} fusion(f32[4,32,1024]{2,1,0:T(8,128)S(1)} %bitcast.60, f32[4,256,32]{1,2,0:T(8,128)S(1)} %get-tuple-element.284), kind=kOutput, calls=%fused_computation.56.clone.1 | convolution fusion | flops 402653184 | bytes 4849664 | tf_op jit(solution)/shard_map/while/body/eval_jaxpr/skd,sdn->skn/dot_general | solution.py:37
  116.2 3.0 fusion.42
  119.2 0.0 copy-start
  119.2 6.5 %fusion.44 = f32[4,256,32]{1,2,0:T(8,128)S(1)} fusion(f32[4,32,1024]{2,1,0:T(8,128)S(1)} %bitcast.61, f32[4,256,1024]{2,1,0:T(8,128)} %get-tuple-element.256, f32[1024]{0:T(1024)S(1)} %dynamic_slice.20, f32[4,1024]{1,0:T(4,128)S(1)} %get-tuple-element.257, f32[4,256,32]{1,2,0:T(8,128)S(1)} %get-tuple-element.271, pred[]{:T(512)S(6)} %compare.6), kind=kOutput, calls=%fused_computation.15.clone.1 | convolution fusion | flops 404815872 | bytes 5001217 | tf_op jit(solution)/shard_map/while/body/eval_jaxpr/skn,sdn->skd/dot_general | solution.py:45
  125.8 0.0 copy-done
  125.8 0.5 fusion.43
  126.4 0.2 copy.31
  126.6 3.5 %fusion.41 = f32[4,1024,256]{1,2,0:T(8,128)S(1)} fusion(f32[4,32,1024]{2,1,0:T(8,128)S(1)} %bitcast.60, f32[4,256,32]{1,2,0:T(8,128)S(1)} %get-tuple-element.284), kind=kOutput, calls=%fused_computation.56.clone.1 | convolution fusion | flops 402653184 | bytes 4849664 | tf_op jit(solution)/shard_map/while/body/eval_jaxpr/skd,sdn->skn/dot_general | solution.py:37
  130.0 3.0 fusion.42
  133.0 0.0 copy-start
  133.0 6.5 %fusion.44 = f32[4,256,32]{1,2,0:T(8,128)S(1)} fusion(f32[4,32,1024]{2,1,0:T(8,128)S(1)} %bitcast.61, f32[4,256,1024]{2,1,0:T(8,128)} %get-tuple-element.256, f32[1024]{0:T(1024)S(1)} %dynamic_slice.20, f32[4,1024]{1,0:T(4,128)S(1)} %get-tuple-element.257, f32[4,256,32]{1,2,0:T(8,128)S(1)} %get-tuple-element.271, pred[]{:T(512)S(6)} %compare.6), kind=kOutput, calls=%fused_computation.15.clone.1 | convolution fusion | flops 404815872 | bytes 5001217 | tf_op jit(solution)/shard_map/while/body/eval_jaxpr/skn,sdn->skd/dot_general | solution.py:45
  139.6 0.0 copy-done
  139.6 0.5 fusion.43
  140.1 0.0 copy-start.3
  140.1 0.6 copy-done.3
  140.8 0.0 all-reduce.3.cloned.1.call-update
  140.8 0.0 all-reduce.5.cloned.1.call-start
  140.8 8.2 %psum.30 = f32[4,256]{1,0:T(4,128)S(1)} all-reduce(f32[4,256]{1,0:T(4,128)S(1)} %get-tuple-element.131), channel_id=1, replica_groups=mesh['list'=16,'sub'=8,'slab'=4] {'slab'}, use_global_device_ids=true, to_apply=%region_12.13 | all-reduce | flops 1024 | bytes 8192 | tf_op jit(solution)/shard_map/psum | solution.py:90
  149.1 28.2 %psum.31 = f32[4,256]{1,0:T(4,128)S(1)} all-reduce(f32[4,256]{1,0:T(4,128)S(1)} %psum.30), channel_id=1, replica_groups=mesh['list'=16,'sub'=8,'slab'=4] {'list'}, use_global_device_ids=true, to_apply=%region_13.14 | all-reduce | flops 1024 | bytes 8192 | tf_op jit(solution)/shard_map/psum | solution.py:90
  177.3 8.0 %all-reduce.3.cloned.1.call-done = f32[4,256,32]{1,2,0:T(8,128)} async-done(((f32[4,256,32]{1,2,0:T(8,128)}), f32[4,256,32]{1,2,0:T(8,128)}) %all-reduce.3.cloned.1.call-update) | async-done | bytes 131088 | tf_op jit(solution)/shard_map/psum | solution.py:90
  185.3 0.0 all-reduce.5.cloned.1.call-update
  185.4 118.7 %all-reduce.5.cloned.1.call-done = f32[4,256,32]{1,2,0:T(8,128)} async-done(((f32[4,256,32]{1,2,0:T(8,128)}), f32[4,256,32]{1,2,0:T(8,128)}) %all-reduce.5.cloned.1.call-update) | async-done | bytes 131088 | tf_op jit(solution)/shard_map/psum | solution.py:90
  304.0 1.6 add_divide_fusion
  (15 shorter events, 0.2 us)
Async XLA Ops:
  9.4 24.8 %all-to-all-start.2 = ((f32[8,64,4]{0,2,1:T(4,128)}), f32[8,64,4]{0,2,1:T(4,128)S(1)}, u32[]{:S(2)}, u32[]{:S(2)}) async-start(f32[8,64,4]{0,2,1:T(4,128)} %broadcast_in_dim.61), calls=%async_computation.2 | async-start | bytes 262144 | tf_op jit(solution)/shard_map/all_to_all | solution.py:77
  28.1 57.1 %copy-start.2 = (bf16[128,4096]{1,0:T(8,128)(2,1)S(1)}, bf16[128,4096]{1,0:T(8,128)(2,1)}, u32[]{:S(2)}) copy-start(bf16[128,4096]{1,0:T(8,128)(2,1)} %param.7) | copy-start | bytes 3145732
  34.2 33.8 %all-to-all-start = ((f32[1024,64,4]{0,2,1:T(4,128)}), f32[1024,64,4]{0,2,1:T(4,128)S(1)}, u32[]{:S(2)}, u32[]{:S(2)}) async-start(f32[1024,64,4]{0,2,1:T(4,128)} %all_to_all.34), calls=%async_computation | async-start | bytes 2097152 | tf_op jit(solution)/shard_map/all_to_all | solution.py:76
  68.0 13.4 %all-to-all-start.3 = ((f32[8,1,256]{2,1,0:T(1,128)}), f32[8,1,256]{2,1,0:T(1,128)S(1)}, u32[]{:S(2)}, u32[]{:S(2)}) async-start(f32[8,1,256]{2,1,0:T(1,128)} %copy.26), calls=%async_computation.3 | async-start | bytes 16384 | tf_op jit(solution)/shard_map/all_to_all | solution.py:81
  74.8 11.1 %copy-start.1 = (f32[4,256,32]{1,2,0:T(8,128)S(1)}, f32[4,256,32]{1,2,0:T(8,128)}, u32[]{:S(2)}) copy-start(f32[4,256,32]{1,2,0:T(8,128)} %param.8) | copy-start | bytes 393220
  81.4 30.4 %all-to-all-start.1 = ((f32[8,128,256]{1,2,0:T(8,128)}), f32[8,128,256]{1,2,0:T(8,128)S(1)}, u32[]{:S(2)}, u32[]{:S(2)}) async-start(f32[8,128,256]{1,2,0:T(8,128)} %copy.25), calls=%async_computation.1 | async-start | bytes 2097152 | tf_op jit(solution)/shard_map/all_to_all | solution.py:80
  84.9 100.4 %all-reduce.3.cloned.1.call-start = ((), (), s32[]{:S(2)}) async-start(), calls=%async_computation.4 | async-start | bytes 262144 | tf_op jit(solution)/shard_map/psum | solution.py:90
  119.2 6.5 %copy-start = (f32[4,256,1024]{2,1,0:T(8,128)S(1)}, f32[4,256,1024]{2,1,0:T(8,128)}, u32[]{:S(2)}) copy-start(f32[4,256,1024]{2,1,0:T(8,128)} %get-tuple-element.256) | copy-start | bytes 12582916 | tf_op jit(solution)/shard_map/while
  133.0 6.5 %copy-start = (f32[4,256,1024]{2,1,0:T(8,128)S(1)}, f32[4,256,1024]{2,1,0:T(8,128)}, u32[]{:S(2)}) copy-start(f32[4,256,1024]{2,1,0:T(8,128)} %get-tuple-element.256) | copy-start | bytes 12582916 | tf_op jit(solution)/shard_map/while
  140.1 0.7 copy-start.3
  140.8 163.3 %all-reduce.5.cloned.1.call-start = ((), (), s32[]{:S(2)}) async-start(), calls=%async_computation.5 | async-start | bytes 262144 | tf_op jit(solution)/shard_map/psum | solution.py:90
Sparse Core Ops, SparseCore 0:
  140.9 44.3 all-reduce.2
  187.8 116.2 all-reduce.4
